TPU v7x, 32 devices: a whole 2x2x4 slice. The times are simulated.
32 devices in a mesh: dp: 2 (over core), expert: 16 (over z, y, x).
Axes of the slice: x: 2, y: 2, z: 4, core: 2. Of those that a mesh axis runs over, the one named last changes fastest.
Arguments:
- tokens: bfloat16 [4096, 2048], P(('dp', 'expert')), may hold values from -6 to 6
- out_grad: bfloat16 [4096, 2048], P(('dp', 'expert')), may hold values from -6 to 6
- expert_ids: int32 [4096, 4], P(('dp', 'expert')), may hold values from 0 to 15, as said below
- gate_weights: float32 [4096, 4], P(('dp', 'expert')), may hold values from 0.05 to 0.6
- w_in: bfloat16 [16, 2048, 768], P('expert'), may hold values from -0.125 to 0.125
- w_out: bfloat16 [16, 384, 2048], P('expert'), may hold values from -0.3125 to 0.3125
Outputs:
- token_grad: bfloat16 [4096, 2048], P(('dp', 'expert'))
- w_in_grad: bfloat16 [16, 2048, 768], P('expert', 'dp')
- w_out_grad: bfloat16 [16, 384, 2048], P('expert', None, 'dp')
Inputs may be any that keep to these rules, and one draw needn't show every extreme that they name: `expert_ids`: each token names 4 different experts; among the 128 tokens of one device no expert is named more than 56 times, and in every device's tokens some expert is named exactly 56 times.
All inputs are finite; a program needn't handle non-finite values.
Results may differ from a plain program's by a relative error of at most 0.0065.
Values may be sent and summed in bfloat16 or wider, within the bound.
A program may use at most 128 MiB of HBM per device.

v0:
```python
import functools
import jax
import jax.numpy as jnp
from jax import lax
from jax.experimental import pallas as pl
from jax.experimental.pallas import tpu as pltpu
from jax.sharding import PartitionSpec as P


def silu_parts(gate_part):
    sigma = 1.0 / (1.0 + jnp.exp(-gate_part))
    return (gate_part * sigma, sigma * (1.0 + gate_part * (1.0 - sigma)))


def backward_rows(rows_in, rows_grad, weight_in, weight_out):
    hidden_width = weight_out.shape[0]
    joined = jnp.dot(rows_in, weight_in, preferred_element_type=jnp.float32)
    gate_part = joined[:, :hidden_width]
    up_part = joined[:, hidden_width:]
    activated, derivative = silu_parts(gate_part)
    hidden = (activated * up_part).astype(jnp.bfloat16)
    d_hidden = lax.dot_general(
        rows_grad, weight_out, (((1,), (1,)), ((), ())), preferred_element_type=jnp.float32
    )
    d_joined = jnp.concatenate(
        [d_hidden * up_part * derivative, d_hidden * activated], axis=1
    ).astype(jnp.bfloat16)
    d_rows = lax.dot_general(
        d_joined, weight_in, (((1,), (1,)), ((), ())), preferred_element_type=jnp.float32
    ).astype(jnp.bfloat16)
    grad_in = lax.dot_general(
        rows_in, d_joined, (((0,), (0,)), ((), ())), preferred_element_type=jnp.float32
    )
    grad_out = lax.dot_general(
        hidden, rows_grad, (((0,), (0,)), ((), ())), preferred_element_type=jnp.float32
    )
    return (d_rows, grad_in, grad_out)


def selection(ids, weights, experts, capacity):
    count = ids.shape[0]
    hit = ids[:, :, None] == experts[None, None, :]
    member = jnp.any(hit, axis=1)
    weight = jnp.sum(jnp.where(hit, weights[:, :, None], 0.0), axis=1)
    earlier = (
        jnp.arange(count, dtype=jnp.int32)[:, None] > jnp.arange(count, dtype=jnp.int32)[None, :]
    ).astype(jnp.bfloat16)
    rank = jnp.dot(earlier, member.astype(jnp.bfloat16), preferred_element_type=jnp.float32)
    rank = jnp.where(member, rank.astype(jnp.int32), -1)
    chosen = rank.T[:, None, :] == jnp.arange(capacity, dtype=jnp.int32)[None, :, None]
    slot_weight = jnp.sum(jnp.where(chosen, weight.T[:, None, :], 0.0), axis=2)
    return chosen.astype(jnp.bfloat16), slot_weight


PLANES = 4
INNER = 4
MESH = pl.DeviceIdType.MESH


def flipped(p, d):
    x, y = p % 2, p // 2
    if d % 2:
        x = 1 - x
    if d // 2:
        y = 1 - y
    return 2 * y + x


def fused_kernel(
    capacity,
    tok_ref,
    og_ref,
    meta_ref,
    w_in_ref,
    w_out_ref,
    tg_ref,
    gin_ref,
    gout_ref,
    ztok,
    zog,
    zmeta,
    send_in,
    send_gr,
    got_in,
    got_gr,
    d_rows,
    ret,
    hid,
    dj,
    part,
    part_got,
    peer_in,
    peer_out,
    far_in,
    far_out,
    z_send,
    z_recv,
    meta_send,
    meta_recv,
    p_send,
    p_recv,
    r_send,
    r_recv,
    t_send,
    t_recv,
    g_send,
    g_recv,
):
    me = lax.axis_index("expert")
    core = lax.axis_index("dp")
    z, p = me // INNER, me % INNER
    count, width = tok_ref.shape
    ff = w_out_ref.shape[0]
    rows = 2 * capacity
    block_rows = INNER * rows
    wide = 512
    odd = z % 2
    pair = z // 2
    partner = z + 1 - 2 * odd
    is_inner = jnp.logical_or(z == 1, z == 2)
    near = 2 - pair
    far = 3 * (1 - pair)
    zdev = lambda s: {"expert": s * INNER + p}
    pdev = lambda d: {"expert": z * INNER + flipped(p, d)}

    def remote(src, dst, send_sem, recv_sem, device):
        return pltpu.make_async_remote_copy(
            src_ref=src,
            dst_ref=dst,
            send_sem=send_sem,
            recv_sem=recv_sem,
            device_id=device,
            device_id_type=MESH,
        )

    barrier = pltpu.get_barrier_semaphore()
    for k in range(1, PLANES):
        pl.semaphore_signal(barrier, inc=1, device_id=zdev((z + k) % PLANES), device_id_type=MESH)
    for d in range(1, INNER):
        pl.semaphore_signal(barrier, inc=1, device_id=pdev(d), device_id_type=MESH)
    pl.semaphore_signal(barrier, inc=1, device_id={"dp": 1 - core}, device_id_type=MESH)
    pl.semaphore_wait(barrier, PLANES + INNER - 1)

    held = (ztok, zog)
    own = (tok_ref, og_ref)

    def meta_copy(s):
        return remote(meta_ref, zmeta.at[z], meta_send.at[s], meta_recv.at[z], zdev(s))

    def arrive_meta(s):
        remote(meta_ref, zmeta.at[s], meta_send.at[s], meta_recv.at[s], zdev(s)).wait_recv()

    def own_copy(a, k, to):
        return remote(own[a], held[a].at[z], z_send.at[a, k], z_recv.at[a, z], zdev(to))

    def pass_on(a, k, s, to):
        return remote(held[a].at[s], held[a].at[s], z_send.at[a, k], z_recv.at[a, s], zdev(to))

    def arrive(a, s):
        remote(held[a].at[s], held[a].at[s], z_send.at[a, 0], z_recv.at[a, s], zdev(s)).wait_recv()

    others = [(z + k) % PLANES for k in range(1, PLANES)]
    cross = near
    for s in others:
        meta_copy(s).start()
    for a in range(2):
        own_copy(a, 0, partner).start()

        @pl.when(is_inner)
        def _():
            own_copy(a, 1, cross).start()

    ztok[z] = tok_ref[...]
    zog[z] = og_ref[...]
    zmeta[z] = meta_ref[...]

    row_id = lax.broadcasted_iota(jnp.int32, (rows, count), 0).astype(jnp.float32)

    def planes_of(b):
        first = 2 * pair if b == 0 else 2 * (1 - pair)
        return (first, first + 1)

    def chosen(s, half, d):
        expert = z * INNER + flipped(p, d)
        code = zmeta[s, pl.ds(expert, 1), :]
        return row_id == code + float(half * capacity)

    def plane_copy(a, b, d):
        src = (send_in, send_gr)[a]
        dst = (got_in, got_gr)[a]
        at = pl.ds(b * block_rows + d * rows, rows)
        return remote(src.at[at], dst.at[at], p_send.at[a, b, d], p_recv.at[a, b, d], pdev(d))

    def dispatch(a, b):
        lo, hi = planes_of(b)
        for d in (3, 1, 2, 0):
            pick_lo, pick_hi = chosen(lo, 0, d), chosen(hi, 1, d)
            sel_lo, sel_hi = pick_lo.astype(jnp.bfloat16), pick_hi.astype(jnp.bfloat16)
            if a == 1:
                expert = z * INNER + flipped(p, d)
                scale = jnp.sum(
                    jnp.where(pick_lo, zmeta[lo, pl.ds(expert + PLANES * INNER, 1), :], 0.0)
                    + jnp.where(pick_hi, zmeta[hi, pl.ds(expert + PLANES * INNER, 1), :], 0.0),
                    axis=1,
                    keepdims=True,
                )
            out = ((got_in, got_gr) if d == 0 else (send_in, send_gr))[a]
            at = pl.ds(b * block_rows + d * rows, rows)

            @pl.loop(0, width // wide)
            def _(c):
                cols = pl.ds(pl.multiple_of(c * wide, wide), wide)
                picked = jnp.dot(
                    sel_lo, held[a][lo, :, cols], preferred_element_type=jnp.float32
                ) + jnp.dot(sel_hi, held[a][hi, :, cols], preferred_element_type=jnp.float32)
                if a == 1:
                    picked = picked * scale
                out[at, cols] = picked.astype(jnp.bfloat16)

            if d:
                plane_copy(a, b, d).start()

    arrive(0, partner)

    @pl.when(is_inner)
    def _():
        pass_on(0, 2, partner, cross).start()

    arrive_meta(partner)
    dispatch(0, 0)
    arrive(1, partner)

    @pl.when(is_inner)
    def _():
        pass_on(1, 2, partner, cross).start()
        for a in range(2):
            arrive(a, near)
            pass_on(a, 3, near, partner).start()

    dispatch(1, 0)

    @pl.when(is_inner)
    def _():
        for a in range(2):
            arrive(a, far)
            pass_on(a, 4, far, partner).start()

    arrive_meta(near)
    arrive_meta(far)
    for a in range(2):

        @pl.when(jnp.logical_not(is_inner))
        def _():
            arrive(a, near)
            arrive(a, far)

        dispatch(a, 1)

    def back_rows(b):
        for a in range(2):
            for d in range(1, INNER):
                plane_copy(a, b, d).wait_recv()
        tile = block_rows // 2

        @pl.loop(0, 2)
        def _(t):
            at = pl.ds(pl.multiple_of(b * block_rows + t * tile, 16), tile)
            joined = jnp.dot(got_in[at, :], w_in_ref[...], preferred_element_type=jnp.float32)
            gate_part, up_part = joined[:, :ff], joined[:, ff:]
            activated, derivative = silu_parts(gate_part)
            hid[at, :] = (activated * up_part).astype(jnp.bfloat16)
            d_hidden = lax.dot_general(
                got_gr[at, :],
                w_out_ref[...],
                (((1,), (1,)), ((), ())),
                preferred_element_type=jnp.float32,
            )
            dj[at, :ff] = (d_hidden * up_part * derivative).astype(jnp.bfloat16)
            dj[at, ff:] = (d_hidden * activated).astype(jnp.bfloat16)

            @pl.loop(0, width // wide)
            def _(c):
                cols = pl.ds(pl.multiple_of(c * wide, wide), wide)
                d_rows[at, cols] = lax.dot_general(
                    dj[at, :],
                    w_in_ref[cols, :],
                    (((1,), (1,)), ((), ())),
                    preferred_element_type=jnp.float32,
                ).astype(jnp.bfloat16)

    def back_copy(b, d):
        at = pl.ds(b * block_rows + d * rows, rows)
        return remote(d_rows.at[at], ret.at[at], r_send.at[b, d], r_recv.at[b, d], pdev(d))

    def part_copy(s):
        return remote(part.at[s], part_got.at[z], t_send.at[s], t_recv.at[z], zdev(s))

    def combine(b, half):
        s = planes_of(b)[half]
        sels = [chosen(s, half, d).astype(jnp.bfloat16) for d in range(INNER)]

        @pl.loop(0, width // wide)
        def _(c):
            cols = pl.ds(pl.multiple_of(c * wide, wide), wide)
            total = jnp.zeros((count, wide), jnp.float32)
            for d in range(INNER):
                at = pl.ds(b * block_rows + d * rows, rows)
                total = total + lax.dot_general(
                    sels[d],
                    (ret if d else d_rows)[at, cols],
                    (((0,), (0,)), ((), ())),
                    preferred_element_type=jnp.float32,
                )
            part[s, :, cols] = total.astype(jnp.bfloat16)

    back_rows(0)
    back_rows(1)
    for b in (1, 0):
        for d in (3, 1, 2):
            back_copy(b, d).start()

    half_width = width // 2
    tile = 256

    def weight_tiles(cols):
        to_in = lax.dot_general(
            got_in[:, cols], dj[...], (((0,), (0,)), ((), ())), preferred_element_type=jnp.float32
        )
        to_out = lax.dot_general(
            hid[...], got_gr[:, cols], (((0,), (0,)), ((), ())), preferred_element_type=jnp.float32
        )
        return to_in, to_out

    @pl.loop(0, half_width // tile)
    def _(c):
        at = pl.ds(pl.multiple_of(c * tile, tile), tile)
        cols = pl.ds(pl.multiple_of((1 - core) * half_width + c * tile, tile), tile)
        to_in, to_out = weight_tiles(cols)
        peer_in[at, :] = to_in
        peer_out[:, at] = to_out

    swaps = [
        remote(peer_in, far_in, g_send.at[0], g_recv.at[0], {"dp": 1 - core}),
        remote(peer_out, far_out, g_send.at[1], g_recv.at[1], {"dp": 1 - core}),
    ]
    for copy in swaps:
        copy.start()

    for d in range(1, INNER):
        back_copy(1, d).wait_recv()
    for half, s in enumerate(planes_of(1)):
        combine(1, half)
        part_copy(s).start()

    for copy in swaps:
        copy.wait_recv()

    @pl.loop(0, half_width // tile)
    def _(c):
        at = pl.ds(pl.multiple_of(c * tile, tile), tile)
        cols = pl.ds(pl.multiple_of(core * half_width + c * tile, tile), tile)
        to_in, to_out = weight_tiles(cols)
        gin_ref[at, :] = (to_in + far_in[at, :]).astype(jnp.bfloat16)
        gout_ref[:, at] = (to_out + far_out[:, at]).astype(jnp.bfloat16)

    for d in range(1, INNER):
        back_copy(0, d).wait_recv()
    for half in range(2):
        combine(0, half)
    part_copy(partner).start()

    for s in others:
        remote(part.at[s], part_got.at[s], t_send.at[s], t_recv.at[s], zdev(s)).wait_recv()

    @pl.loop(0, width // wide)
    def _(c):
        cols = pl.ds(pl.multiple_of(c * wide, wide), wide)
        total = part[z, :, cols].astype(jnp.float32)
        for s in others:
            total = total + part_got[s, :, cols].astype(jnp.float32)
        tg_ref[:, cols] = total.astype(jnp.bfloat16)

    for s in others:
        meta_copy(s).wait_send()
        part_copy(s).wait_send()
    for a in range(2):
        own_copy(a, 0, partner).wait_send()

        @pl.when(is_inner)
        def _():
            own_copy(a, 1, cross).wait_send()
            pass_on(a, 2, partner, cross).wait_send()
            pass_on(a, 3, near, partner).wait_send()
            pass_on(a, 4, far, partner).wait_send()

    for b in range(2):
        for d in range(1, INNER):
            for a in range(2):
                plane_copy(a, b, d).wait_send()
            back_copy(b, d).wait_send()
    for copy in swaps:
        copy.wait_send()


def fused(capacity, tokens, out_grad, expert_ids, gate_weights, w_in, w_out):
    hosts = PLANES * INNER
    count, width = tokens.shape
    ff = w_out.shape[1]
    hit = expert_ids.T[:, None, :] == jnp.arange(hosts, dtype=jnp.int32)[None, :, None]
    member = jnp.any(hit, axis=0)
    weight = jnp.sum(jnp.where(hit, gate_weights.T[:, None, :], 0.0), axis=0)
    order = jnp.arange(count, dtype=jnp.int32)
    earlier = (order[:, None] < order[None, :]).astype(jnp.bfloat16)
    rank = jnp.dot(member.astype(jnp.bfloat16), earlier, preferred_element_type=jnp.float32)
    code = jnp.where(member, rank, -1024.0)
    meta = jnp.concatenate([code, weight], axis=0)
    slots = 2 * INNER * 2 * capacity
    vmem = pl.BlockSpec(memory_space=pltpu.VMEM)
    bf16, f32, dma = jnp.bfloat16, jnp.float32, pltpu.SemaphoreType.DMA
    token_grad, grad_in, grad_out = pl.pallas_call(
        functools.partial(fused_kernel, capacity),
        out_shape=[
            jax.ShapeDtypeStruct((count, width), bf16),
            jax.ShapeDtypeStruct((width // 2, 2 * ff), bf16),
            jax.ShapeDtypeStruct((ff, width // 2), bf16),
        ],
        in_specs=[vmem] * 5,
        out_specs=[vmem] * 3,
        scratch_shapes=[
            pltpu.VMEM((PLANES, count, width), bf16),
            pltpu.VMEM((PLANES, count, width), bf16),
            pltpu.VMEM((PLANES, 2 * hosts, count), f32),
            pltpu.VMEM((slots, width), bf16),
            pltpu.VMEM((slots, width), bf16),
            pltpu.VMEM((slots, width), bf16),
            pltpu.VMEM((slots, width), bf16),
            pltpu.VMEM((slots, width), bf16),
            pltpu.VMEM((slots, width), bf16),
            pltpu.VMEM((slots, ff), bf16),
            pltpu.VMEM((slots, 2 * ff), bf16),
            pltpu.VMEM((PLANES, count, width), bf16),
            pltpu.VMEM((PLANES, count, width), bf16),
            pltpu.VMEM((width // 2, 2 * ff), f32),
            pltpu.VMEM((ff, width // 2), f32),
            pltpu.VMEM((width // 2, 2 * ff), f32),
            pltpu.VMEM((ff, width // 2), f32),
            dma((2, 5)),
            dma((2, PLANES)),
            dma((PLANES,)),
            dma((PLANES,)),
            dma((2, 2, INNER)),
            dma((2, 2, INNER)),
            dma((2, INNER)),
            dma((2, INNER)),
            dma((PLANES,)),
            dma((PLANES,)),
            dma((2,)),
            dma((2,)),
        ],
        compiler_params=pltpu.CompilerParams(
            collective_id=0, has_side_effects=True, vmem_limit_bytes=60 * 2**20
        ),
        cost_estimate=pl.CostEstimate(
            flops=2 * slots * width * ff * 8, bytes_accessed=12 * 2**20, transcendentals=slots * ff
        ),
    )(tokens, out_grad, meta, w_in[0], w_out[0])
    return token_grad, grad_in[None], grad_out[None]


def body(tokens, out_grad, expert_ids, gate_weights, w_in, w_out):
    hosts = lax.axis_size("expert")
    token_count, model_width = tokens.shape
    capacity = 7 * token_count * expert_ids.shape[1] // (4 * hosts)
    if hosts == 16 and 2 * capacity % 16 == 0:
        return fused(capacity, tokens, out_grad, expert_ids, gate_weights, w_in, w_out)
    pick, slot_weight = selection(
        expert_ids, gate_weights, jnp.arange(hosts, dtype=jnp.int32), capacity
    )
    pick = pick.reshape(hosts * capacity, token_count)
    send_in = jnp.dot(pick, tokens, preferred_element_type=jnp.float32).astype(jnp.bfloat16)
    send_grad = (
        slot_weight.reshape(-1, 1) * jnp.dot(pick, out_grad, preferred_element_type=jnp.float32)
    ).astype(jnp.bfloat16)
    got_in = lax.all_to_all(send_in, "expert", split_axis=0, concat_axis=0, tiled=True)
    got_grad = lax.all_to_all(send_grad, "expert", split_axis=0, concat_axis=0, tiled=True)
    d_rows, grad_in, grad_out = backward_rows(got_in, got_grad, w_in[0], w_out[0])
    returned = lax.all_to_all(d_rows, "expert", split_axis=0, concat_axis=0, tiled=True)
    sum_in = lax.psum_scatter(grad_in, "dp", scatter_dimension=0, tiled=True)
    sum_out = lax.psum_scatter(grad_out, "dp", scatter_dimension=1, tiled=True)
    token_grad = lax.dot_general(
        pick, returned, (((0,), (0,)), ((), ())), preferred_element_type=jnp.float32
    ).astype(jnp.bfloat16)
    return (token_grad, sum_in.astype(jnp.bfloat16)[None], sum_out.astype(jnp.bfloat16)[None])


def solution(mesh):
    in_specs = (
        P(("dp", "expert"), None),
        P(("dp", "expert"), None),
        P(("dp", "expert"), None),
        P(("dp", "expert"), None),
        P("expert", None, None),
        P("expert", None, None),
    )
    out_specs = (P(("dp", "expert"), None), P("expert", "dp", None), P("expert", None, "dp"))
    return jax.shard_map(body, mesh=mesh, in_specs=in_specs, out_specs=out_specs, check_vma=False)
```

profile of v0, /device:TPU:25, one launch (start us, length us, event | category | flops | bytes accessed | tf_op | source)
XLA Modules:
  0.0 193.9 jit_solution(9692357071936760673)
XLA Ops:
  0.6 0.7 fusion
  1.3 0.1 convolution_select_fusion
  1.5 0.7 select_reduce_fusion
  2.2 0.6 pad_maximum_fusion.meta_ref
  2.8 185.6 %shard_map.85 = (bf16[128,2048]{1,0:T(8,128)(2,1)}, bf16[1024,768]{1,0:T(8,128)(2,1)}, bf16[384,1024]{1,0:T(8,128)(2,1)}) custom-call(bf16[128,2048]{1,0:T(8,128)(2,1)} %tok_ref.1, bf16[128,2048]{1,0:T(8,128)(2,1)} %og_ref.1, f32[32,128]{1,0:T(8,128)} %pad_maximum_fusion.meta_ref, bf16[2048,768]{1,0:T(8,128)(2,1)} %bitcast.12, bf16[384,2048]{1,0:T(8,128)(2,1)} %bitcast.13), custom_call_target="tpu_custom_call" | custom-call | flops 11274289152 | bytes 12582912 | tf_op jit(solution)/shard_map/pallas_call | solution.py:420
  188.4 1.9 copy.12
  190.3 0.0 copy-start
  190.3 2.7 %copy.13 = bf16[1,1024,768]{2,1,0:T(8,128)(2,1)} copy(bf16[1,1024,768]{2,1,0:T(8,128)(2,1)} %bitcast.7) | data formatting | bytes 3145728
  193.0 0.0 copy-done
  193.0 0.9 copy.14
Async XLA Ops:
  190.3 2.7 %copy-start = (bf16[384,1024]{1,0:T(8,128)(2,1)S(1)}, bf16[384,1024]{1,0:T(8,128)(2,1)}, u32[]{:S(2)}) copy-start(bf16[384,1024]{1,0:T(8,128)(2,1)} %get-tuple-element.8) | copy-start | bytes 2359300
where the time goes:
time: 194 us
  Pallas kernels  186 us (96%)
  local copies, waits for them, and re-layouts  5.49 us (3%)
  other arithmetic  2.01 us (1%)
    pallas_call x1, Pallas kernels, fused(): pl.pallas_call(functools.partial(fused_kernel, capacity), out_shape=[jax....  186 us
    unnamed x5, local copies, waits for them, and re-layouts  5.49 us

commit v1 on v0

--- a/solution.py
+++ b/solution.py
@@ -71,11 +71,16 @@
     tok_ref,
     og_ref,
     meta_ref,
+    w_in_hbm,
+    w_out_hbm,
+    tg_ref,
+    gin_hbm,
+    gout_hbm,
     w_in_ref,
     w_out_ref,
-    tg_ref,
     gin_ref,
     gout_ref,
+    joined_ref,
     ztok,
     zog,
     zmeta,
@@ -105,6 +110,7 @@
     t_recv,
     g_send,
     g_recv,
+    local_sem,
 ):
     me = lax.axis_index("expert")
     core = lax.axis_index("dp")
@@ -133,6 +139,14 @@
             device_id_type=MESH,
         )
 
+    loads = [
+        pltpu.make_async_copy(w_in_hbm, w_in_ref, local_sem.at[0]),
+        pltpu.make_async_copy(w_out_hbm, w_out_ref, local_sem.at[1]),
+    ]
+    stores = [
+        pltpu.make_async_copy(gin_ref, gin_hbm, local_sem.at[2]),
+        pltpu.make_async_copy(gout_ref, gout_hbm, local_sem.at[3]),
+    ]
     barrier = pltpu.get_barrier_semaphore()
     for k in range(1, PLANES):
         pl.semaphore_signal(barrier, inc=1, device_id=zdev((z + k) % PLANES), device_id_type=MESH)
@@ -170,6 +184,8 @@
         def _():
             own_copy(a, 1, cross).start()
 
+    for copy in loads:
+        copy.start()
     ztok[z] = tok_ref[...]
     zog[z] = og_ref[...]
     zmeta[z] = meta_ref[...]
@@ -177,48 +193,60 @@
     row_id = lax.broadcasted_iota(jnp.int32, (rows, count), 0).astype(jnp.float32)
 
     def planes_of(b):
-        first = 2 * pair if b == 0 else 2 * (1 - pair)
-        return (first, first + 1)
+        return (z, partner) if b == 0 else (near, far)
 
     def chosen(s, half, d):
         expert = z * INNER + flipped(p, d)
         code = zmeta[s, pl.ds(expert, 1), :]
         return row_id == code + float(half * capacity)
 
-    def plane_copy(a, b, d):
+    ready = capacity // 16 * 16
+    pieces = ((0, 0, ready), (0, ready, rows - ready), (1, 0, rows))
+
+    def plane_copy(a, piece, d):
+        b, start, size = pieces[piece]
         src = (send_in, send_gr)[a]
         dst = (got_in, got_gr)[a]
-        at = pl.ds(b * block_rows + d * rows, rows)
-        return remote(src.at[at], dst.at[at], p_send.at[a, b, d], p_recv.at[a, b, d], pdev(d))
-
-    def dispatch(a, b):
-        lo, hi = planes_of(b)
+        at = pl.ds(b * block_rows + d * rows + start, size)
+        return remote(
+            src.at[at], dst.at[at], p_send.at[a, piece, d], p_recv.at[a, piece, d], pdev(d)
+        )
+
+    def dispatch(a, piece):
+        b, start, size = pieces[piece]
+        planes = planes_of(b)[: 1 if piece == 0 else 2]
         for d in (3, 1, 2, 0):
-            pick_lo, pick_hi = chosen(lo, 0, d), chosen(hi, 1, d)
-            sel_lo, sel_hi = pick_lo.astype(jnp.bfloat16), pick_hi.astype(jnp.bfloat16)
+            picks = [chosen(s, half, d)[start : start + size] for half, s in enumerate(planes)]
+            sels = [pick.astype(jnp.bfloat16) for pick in picks]
             if a == 1:
-                expert = z * INNER + flipped(p, d)
+                expert = z * INNER + flipped(p, d) + PLANES * INNER
                 scale = jnp.sum(
-                    jnp.where(pick_lo, zmeta[lo, pl.ds(expert + PLANES * INNER, 1), :], 0.0)
-                    + jnp.where(pick_hi, zmeta[hi, pl.ds(expert + PLANES * INNER, 1), :], 0.0),
+                    sum(
+                        jnp.where(pick, zmeta[s, pl.ds(expert, 1), :], 0.0)
+                        for pick, s in zip(picks, planes)
+                    ),
                     axis=1,
                     keepdims=True,
                 )
             out = ((got_in, got_gr) if d == 0 else (send_in, send_gr))[a]
-            at = pl.ds(b * block_rows + d * rows, rows)
+            at = pl.ds(b * block_rows + d * rows + start, size)
 
             @pl.loop(0, width // wide)
             def _(c):
                 cols = pl.ds(pl.multiple_of(c * wide, wide), wide)
-                picked = jnp.dot(
-                    sel_lo, held[a][lo, :, cols], preferred_element_type=jnp.float32
-                ) + jnp.dot(sel_hi, held[a][hi, :, cols], preferred_element_type=jnp.float32)
+                picked = sum(
+                    jnp.dot(sel, held[a][s, :, cols], preferred_element_type=jnp.float32)
+                    for sel, s in zip(sels, planes)
+                )
                 if a == 1:
                     picked = picked * scale
                 out[at, cols] = picked.astype(jnp.bfloat16)
 
             if d:
-                plane_copy(a, b, d).start()
+                plane_copy(a, piece, d).start()
+
+    dispatch(0, 0)
+    dispatch(1, 0)
 
     arrive(0, partner)
 
@@ -227,7 +255,7 @@
         pass_on(0, 2, partner, cross).start()
 
     arrive_meta(partner)
-    dispatch(0, 0)
+    dispatch(0, 1)
     arrive(1, partner)
 
     @pl.when(is_inner)
@@ -237,7 +265,7 @@
             arrive(a, near)
             pass_on(a, 3, near, partner).start()
 
-    dispatch(1, 0)
+    dispatch(1, 1)
 
     @pl.when(is_inner)
     def _():
@@ -254,19 +282,31 @@
             arrive(a, near)
             arrive(a, far)
 
-        dispatch(a, 1)
-
-    def back_rows(b):
-        for a in range(2):
-            for d in range(1, INNER):
-                plane_copy(a, b, d).wait_recv()
-        tile = block_rows // 2
-
+        dispatch(a, 2)
+
+    def arrive_rows(a, b):
+        for d in range(1, INNER):
+            for piece in range(len(pieces)):
+                if pieces[piece][0] == b:
+                    plane_copy(a, piece, d).wait_recv()
+
+    tile_rows = block_rows // 2
+    quarters = width // wide
+
+    def joined_rows(b):
         @pl.loop(0, 2)
         def _(t):
-            at = pl.ds(pl.multiple_of(b * block_rows + t * tile, 16), tile)
-            joined = jnp.dot(got_in[at, :], w_in_ref[...], preferred_element_type=jnp.float32)
-            gate_part, up_part = joined[:, :ff], joined[:, ff:]
+            at = pl.ds(pl.multiple_of(b * block_rows + t * tile_rows, 16), tile_rows)
+            joined_ref[pl.ds(pl.multiple_of(t * tile_rows, 16), tile_rows), :] = jnp.dot(
+                got_in[at, :], w_in_ref[...], preferred_element_type=jnp.float32
+            )
+
+    def hidden_rows(b):
+        @pl.loop(0, 2)
+        def _(t):
+            at = pl.ds(pl.multiple_of(b * block_rows + t * tile_rows, 16), tile_rows)
+            here = pl.ds(pl.multiple_of(t * tile_rows, 16), tile_rows)
+            gate_part, up_part = joined_ref[here, :ff], joined_ref[here, ff:]
             activated, derivative = silu_parts(gate_part)
             hid[at, :] = (activated * up_part).astype(jnp.bfloat16)
             d_hidden = lax.dot_general(
@@ -278,46 +318,66 @@
             dj[at, :ff] = (d_hidden * up_part * derivative).astype(jnp.bfloat16)
             dj[at, ff:] = (d_hidden * activated).astype(jnp.bfloat16)
 
-            @pl.loop(0, width // wide)
-            def _(c):
-                cols = pl.ds(pl.multiple_of(c * wide, wide), wide)
-                d_rows[at, cols] = lax.dot_general(
-                    dj[at, :],
-                    w_in_ref[cols, :],
-                    (((1,), (1,)), ((), ())),
-                    preferred_element_type=jnp.float32,
-                ).astype(jnp.bfloat16)
-
-    def back_copy(b, d):
-        at = pl.ds(b * block_rows + d * rows, rows)
-        return remote(d_rows.at[at], ret.at[at], r_send.at[b, d], r_recv.at[b, d], pdev(d))
-
-    def part_copy(s):
-        return remote(part.at[s], part_got.at[z], t_send.at[s], t_recv.at[z], zdev(s))
-
-    def combine(b, half):
+    def input_rows(b, c):
+        at = pl.ds(b * block_rows, block_rows)
+        cols = pl.ds(c * wide, wide)
+        d_rows[at, cols] = lax.dot_general(
+            dj[at, :],
+            w_in_ref[cols, :],
+            (((1,), (1,)), ((), ())),
+            preferred_element_type=jnp.float32,
+        ).astype(jnp.bfloat16)
+
+    def back_copy(b, d, c):
+        at = (pl.ds(b * block_rows + d * rows, rows), pl.ds(c * wide, wide))
+        return remote(d_rows.at[at], ret.at[at], r_send.at[b, d, c], r_recv.at[b, d, c], pdev(d))
+
+    def part_copy(s, c):
+        cols = pl.ds(c * wide, wide)
+        return remote(
+            part.at[s, :, cols],
+            part_got.at[z, :, cols],
+            t_send.at[s, c],
+            t_recv.at[z, c],
+            zdev(s),
+        )
+
+    def combine(b, half, c):
         s = planes_of(b)[half]
-        sels = [chosen(s, half, d).astype(jnp.bfloat16) for d in range(INNER)]
-
-        @pl.loop(0, width // wide)
-        def _(c):
-            cols = pl.ds(pl.multiple_of(c * wide, wide), wide)
-            total = jnp.zeros((count, wide), jnp.float32)
-            for d in range(INNER):
-                at = pl.ds(b * block_rows + d * rows, rows)
-                total = total + lax.dot_general(
-                    sels[d],
-                    (ret if d else d_rows)[at, cols],
-                    (((0,), (0,)), ((), ())),
-                    preferred_element_type=jnp.float32,
-                )
-            part[s, :, cols] = total.astype(jnp.bfloat16)
-
-    back_rows(0)
-    back_rows(1)
-    for b in (1, 0):
+        cols = pl.ds(c * wide, wide)
+        total = jnp.zeros((count, wide), jnp.float32)
+        for d in range(INNER):
+            at = pl.ds(b * block_rows + d * rows, rows)
+            total = total + lax.dot_general(
+                chosen(s, half, d).astype(jnp.bfloat16),
+                (ret if d else d_rows)[at, cols],
+                (((0,), (0,)), ((), ())),
+                preferred_element_type=jnp.float32,
+            )
+        part[s, :, cols] = total.astype(jnp.bfloat16)
+
+    for copy in loads:
+        copy.wait()
+    arrive_rows(0, 0)
+    joined_rows(0)
+    arrive_rows(1, 0)
+    hidden_rows(0)
+    for c in range(quarters):
+        input_rows(0, c)
+    arrive_rows(0, 1)
+    joined_rows(1)
+    arrive_rows(1, 1)
+    early = [(3, c) for c in range(quarters // 2)]
+    late = [(d, c) for c in range(quarters) for d in (3, 1, 2) if (d, c) not in early]
+    for d, c in early:
+        back_copy(0, d, c).start()
+    hidden_rows(1)
+    for c in range(quarters):
+        input_rows(1, c)
         for d in (3, 1, 2):
-            back_copy(b, d).start()
+            back_copy(1, d, c).start()
+    for d, c in late:
+        back_copy(0, d, c).start()
 
     half_width = width // 2
     tile = 256
@@ -346,11 +406,12 @@
     for copy in swaps:
         copy.start()
 
-    for d in range(1, INNER):
-        back_copy(1, d).wait_recv()
-    for half, s in enumerate(planes_of(1)):
-        combine(1, half)
-        part_copy(s).start()
+    for c in range(quarters):
+        for d in range(1, INNER):
+            back_copy(1, d, c).wait_recv()
+        for half, s in ((1, far), (0, near)):
+            combine(1, half, c)
+            part_copy(s, c).start()
 
     for copy in swaps:
         copy.wait_recv()
@@ -363,26 +424,34 @@
         gin_ref[at, :] = (to_in + far_in[at, :]).astype(jnp.bfloat16)
         gout_ref[:, at] = (to_out + far_out[:, at]).astype(jnp.bfloat16)
 
-    for d in range(1, INNER):
-        back_copy(0, d).wait_recv()
-    for half in range(2):
-        combine(0, half)
-    part_copy(partner).start()
-
-    for s in others:
-        remote(part.at[s], part_got.at[s], t_send.at[s], t_recv.at[s], zdev(s)).wait_recv()
-
-    @pl.loop(0, width // wide)
-    def _(c):
-        cols = pl.ds(pl.multiple_of(c * wide, wide), wide)
+    for copy in stores:
+        copy.start()
+
+    for c in range(quarters):
+        for d in range(1, INNER):
+            back_copy(0, d, c).wait_recv()
+        combine(0, 1, c)
+        part_copy(partner, c).start()
+        combine(0, 0, c)
+
+    for c in range(quarters):
+        cols = pl.ds(c * wide, wide)
         total = part[z, :, cols].astype(jnp.float32)
         for s in others:
+            remote(
+                part.at[s, :, cols],
+                part_got.at[s, :, cols],
+                t_send.at[s, c],
+                t_recv.at[s, c],
+                zdev(s),
+            ).wait_recv()
             total = total + part_got[s, :, cols].astype(jnp.float32)
         tg_ref[:, cols] = total.astype(jnp.bfloat16)
 
     for s in others:
         meta_copy(s).wait_send()
-        part_copy(s).wait_send()
+        for c in range(quarters):
+            part_copy(s, c).wait_send()
     for a in range(2):
         own_copy(a, 0, partner).wait_send()
 
@@ -393,13 +462,17 @@
             pass_on(a, 3, near, partner).wait_send()
             pass_on(a, 4, far, partner).wait_send()
 
-    for b in range(2):
-        for d in range(1, INNER):
-            for a in range(2):
-                plane_copy(a, b, d).wait_send()
-            back_copy(b, d).wait_send()
+    for d in range(1, INNER):
+        for a in range(2):
+            for piece in range(len(pieces)):
+                plane_copy(a, piece, d).wait_send()
+        for b in range(2):
+            for c in range(quarters):
+                back_copy(b, d, c).wait_send()
     for copy in swaps:
         copy.wait_send()
+    for copy in stores:
+        copy.wait()
 
 
 def fused(capacity, tokens, out_grad, expert_ids, gate_weights, w_in, w_out):
@@ -416,6 +489,8 @@
     meta = jnp.concatenate([code, weight], axis=0)
     slots = 2 * INNER * 2 * capacity
     vmem = pl.BlockSpec(memory_space=pltpu.VMEM)
+    hbm = pl.BlockSpec(memory_space=pl.ANY)
+    quarters = width // 512
     bf16, f32, dma = jnp.bfloat16, jnp.float32, pltpu.SemaphoreType.DMA
     token_grad, grad_in, grad_out = pl.pallas_call(
         functools.partial(fused_kernel, capacity),
@@ -424,9 +499,14 @@
             jax.ShapeDtypeStruct((width // 2, 2 * ff), bf16),
             jax.ShapeDtypeStruct((ff, width // 2), bf16),
         ],
-        in_specs=[vmem] * 5,
-        out_specs=[vmem] * 3,
+        in_specs=[vmem] * 3 + [hbm] * 2,
+        out_specs=[vmem, hbm, hbm],
         scratch_shapes=[
+            pltpu.VMEM((width, 2 * ff), bf16),
+            pltpu.VMEM((ff, width), bf16),
+            pltpu.VMEM((width // 2, 2 * ff), bf16),
+            pltpu.VMEM((ff, width // 2), bf16),
+            pltpu.VMEM((slots // 2, 2 * ff), f32),
             pltpu.VMEM((PLANES, count, width), bf16),
             pltpu.VMEM((PLANES, count, width), bf16),
             pltpu.VMEM((PLANES, 2 * hosts, count), f32),
@@ -448,14 +528,15 @@
             dma((2, PLANES)),
             dma((PLANES,)),
             dma((PLANES,)),
-            dma((2, 2, INNER)),
-            dma((2, 2, INNER)),
-            dma((2, INNER)),
-            dma((2, INNER)),
-            dma((PLANES,)),
-            dma((PLANES,)),
+            dma((2, 3, INNER)),
+            dma((2, 3, INNER)),
+            dma((2, INNER, quarters)),
+            dma((2, INNER, quarters)),
+            dma((PLANES, quarters)),
+            dma((PLANES, quarters)),
             dma((2,)),
             dma((2,)),
+            dma((4,)),
         ],
         compiler_params=pltpu.CompilerParams(
             collective_id=0, has_side_effects=True, vmem_limit_bytes=60 * 2**20

time: 194 us -> 165 us (0.85)
  the two profiles are of different devices: /device:TPU:25 before, /device:TPU:0 now
where the time goes in v1:
time: 165 us
  Pallas kernels  156 us (95%)
  local copies, waits for them, and re-layouts  5.49 us (3%)
  other arithmetic  2.01 us (1%)
    pallas_call x1, Pallas kernels, fused(): pl.pallas_call(functools.partial(fused_kernel, capacity), out_shape=[jax....  156 us
    unnamed x5, local copies, waits for them, and re-layouts  5.49 us

profile of v1, /device:TPU:0, one launch (start us, length us, event | category | flops | bytes accessed | tf_op | source)
XLA Modules:
  0.0 164.8 jit_solution(10992203817655065031)
XLA Ops:
  0.6 0.7 fusion
  1.3 0.1 convolution_select_fusion
  1.5 0.7 select_reduce_fusion
  2.2 0.6 pad_maximum_fusion.meta_ref
  2.8 156.5 %shard_map.85 = (bf16[128,2048]{1,0:T(8,128)(2,1)}, bf16[1024,768]{1,0:T(8,128)(2,1)}, bf16[384,1024]{1,0:T(8,128)(2,1)}) custom-call(bf16[128,2048]{1,0:T(8,128)(2,1)} %tok_ref.1, bf16[128,2048]{1,0:T(8,128)(2,1)} %og_ref.1, f32[32,128]{1,0:T(8,128)} %pad_maximum_fusion.meta_ref, bf16[2048,768]{1,0:T(8,128)(2,1)} %bitcast.12, bf16[384,2048]{1,0:T(8,128)(2,1)} %bitcast.13), custom_call_target="tpu_custom_call" | custom-call | flops 11274289152 | bytes 12582912 | tf_op jit(solution)/shard_map/pallas_call | solution.py:495
  159.3 1.9 %copy.12 = bf16[128,2048]{1,0:T(8,128)(2,1)} copy(bf16[128,2048]{1,0:T(8,128)(2,1)} %get-tuple-element.12) | data formatting | bytes 1048576
  161.2 0.0 copy-start
  161.2 2.7 %copy.13 = bf16[1,1024,768]{2,1,0:T(8,128)(2,1)} copy(bf16[1,1024,768]{2,1,0:T(8,128)(2,1)} %bitcast.7) | data formatting | bytes 3145728
  163.9 0.0 copy-done
  163.9 0.9 copy.14
Async XLA Ops:
  161.2 2.7 %copy-start = (bf16[384,1024]{1,0:T(8,128)(2,1)S(1)}, bf16[384,1024]{1,0:T(8,128)(2,1)}, u32[]{:S(2)}) copy-start(bf16[384,1024]{1,0:T(8,128)(2,1)} %get-tuple-element.8) | copy-start | bytes 2359300

commit v2 on v1

--- a/solution.py
+++ b/solution.py
@@ -94,6 +94,7 @@
     dj,
     part,
     part_got,
+    kept,
     peer_in,
     peer_out,
     far_in,
@@ -201,7 +202,7 @@
         return row_id == code + float(half * capacity)
 
     ready = capacity // 16 * 16
-    pieces = ((0, 0, ready), (0, ready, rows - ready), (1, 0, rows))
+    pieces = tuple((b, *cut) for b in range(2) for cut in ((0, ready), (ready, rows - ready)))
 
     def plane_copy(a, piece, d):
         b, start, size = pieces[piece]
@@ -214,7 +215,7 @@
 
     def dispatch(a, piece):
         b, start, size = pieces[piece]
-        planes = planes_of(b)[: 1 if piece == 0 else 2]
+        planes = planes_of(b)[: 1 if start == 0 else 2]
         for d in (3, 1, 2, 0):
             picks = [chosen(s, half, d)[start : start + size] for half, s in enumerate(planes)]
             sels = [pick.astype(jnp.bfloat16) for pick in picks]
@@ -267,12 +268,6 @@
 
     dispatch(1, 1)
 
-    @pl.when(is_inner)
-    def _():
-        for a in range(2):
-            arrive(a, far)
-            pass_on(a, 4, far, partner).start()
-
     arrive_meta(near)
     arrive_meta(far)
     for a in range(2):
@@ -280,9 +275,24 @@
         @pl.when(jnp.logical_not(is_inner))
         def _():
             arrive(a, near)
+
+        dispatch(a, 2)
+
+        if a == 0:
+
+            @pl.when(is_inner)
+            def _():
+                for other in range(2):
+                    arrive(other, far)
+                    pass_on(other, 4, far, partner).start()
+
+    for a in range(2):
+
+        @pl.when(jnp.logical_not(is_inner))
+        def _():
             arrive(a, far)
 
-        dispatch(a, 2)
+        dispatch(a, 3)
 
     def arrive_rows(a, b):
         for d in range(1, INNER):
@@ -332,15 +342,26 @@
         at = (pl.ds(b * block_rows + d * rows, rows), pl.ds(c * wide, wide))
         return remote(d_rows.at[at], ret.at[at], r_send.at[b, d, c], r_recv.at[b, d, c], pdev(d))
 
-    def part_copy(s, c):
+    from_end_near, from_end_far, from_partner, from_cross, from_cross_far = range(5)
+
+    def part_copy(slot, land, to, c):
         cols = pl.ds(c * wide, wide)
         return remote(
-            part.at[s, :, cols],
-            part_got.at[z, :, cols],
-            t_send.at[s, c],
-            t_recv.at[z, c],
-            zdev(s),
+            part.at[slot, :, cols],
+            part_got.at[land, :, cols],
+            t_send.at[slot, c],
+            t_recv.at[land, c],
+            zdev(to),
         )
+
+    def landed(land, c):
+        cols = pl.ds(c * wide, wide)
+        part_copy(0, land, partner, c).wait_recv()
+        return part_got[land, :, cols].astype(jnp.float32)
+
+    def send_part(total, slot, land, to, c):
+        part[slot, :, pl.ds(c * wide, wide)] = total.astype(jnp.bfloat16)
+        part_copy(slot, land, to, c).start()
 
     def combine(b, half, c):
         s = planes_of(b)[half]
@@ -354,7 +375,7 @@
                 (((0,), (0,)), ((), ())),
                 preferred_element_type=jnp.float32,
             )
-        part[s, :, cols] = total.astype(jnp.bfloat16)
+        return total
 
     for copy in loads:
         copy.wait()
@@ -409,9 +430,17 @@
     for c in range(quarters):
         for d in range(1, INNER):
             back_copy(1, d, c).wait_recv()
-        for half, s in ((1, far), (0, near)):
-            combine(1, half, c)
-            part_copy(s, c).start()
+        totals = [combine(1, half, c) for half in range(2)]
+
+        @pl.when(is_inner)
+        def _():
+            for k in range(2):
+                send_part(totals[k] + landed(from_end_near + k, c), k, from_cross + k, near, c)
+
+        @pl.when(jnp.logical_not(is_inner))
+        def _():
+            for k in range(2):
+                send_part(totals[k], k, from_end_near + k, partner, c)
 
     for copy in swaps:
         copy.wait_recv()
@@ -430,28 +459,33 @@
     for c in range(quarters):
         for d in range(1, INNER):
             back_copy(0, d, c).wait_recv()
-        combine(0, 1, c)
-        part_copy(partner, c).start()
-        combine(0, 0, c)
+        total = combine(0, 1, c)
+
+        @pl.when(is_inner)
+        def _():
+            send_part(total + landed(from_cross_far, c), 2, from_partner, partner, c)
+
+        @pl.when(jnp.logical_not(is_inner))
+        def _():
+            send_part(total, 2, from_partner, partner, c)
+
+        kept[:, pl.ds(c * wide, wide)] = combine(0, 0, c)
 
     for c in range(quarters):
         cols = pl.ds(c * wide, wide)
-        total = part[z, :, cols].astype(jnp.float32)
-        for s in others:
-            remote(
-                part.at[s, :, cols],
-                part_got.at[s, :, cols],
-                t_send.at[s, c],
-                t_recv.at[s, c],
-                zdev(s),
-            ).wait_recv()
-            total = total + part_got[s, :, cols].astype(jnp.float32)
-        tg_ref[:, cols] = total.astype(jnp.bfloat16)
+        kept[:, cols] += landed(from_partner, c)
+
+        @pl.when(is_inner)
+        def _():
+            kept[:, cols] += landed(from_cross, c)
+
+        tg_ref[:, cols] = kept[:, cols].astype(jnp.bfloat16)
 
     for s in others:
         meta_copy(s).wait_send()
+    for slot in range(3):
         for c in range(quarters):
-            part_copy(s, c).wait_send()
+            part_copy(slot, from_partner, partner, c).wait_send()
     for a in range(2):
         own_copy(a, 0, partner).wait_send()
 
@@ -518,8 +552,9 @@
             pltpu.VMEM((slots, width), bf16),
             pltpu.VMEM((slots, ff), bf16),
             pltpu.VMEM((slots, 2 * ff), bf16),
-            pltpu.VMEM((PLANES, count, width), bf16),
-            pltpu.VMEM((PLANES, count, width), bf16),
+            pltpu.VMEM((3, count, width), bf16),
+            pltpu.VMEM((5, count, width), bf16),
+            pltpu.VMEM((count, width), f32),
             pltpu.VMEM((width // 2, 2 * ff), f32),
             pltpu.VMEM((ff, width // 2), f32),
             pltpu.VMEM((width // 2, 2 * ff), f32),
@@ -528,12 +563,12 @@
             dma((2, PLANES)),
             dma((PLANES,)),
             dma((PLANES,)),
-            dma((2, 3, INNER)),
-            dma((2, 3, INNER)),
+            dma((2, 4, INNER)),
+            dma((2, 4, INNER)),
             dma((2, INNER, quarters)),
             dma((2, INNER, quarters)),
-            dma((PLANES, quarters)),
-            dma((PLANES, quarters)),
+            dma((3, quarters)),
+            dma((5, quarters)),
             dma((2,)),
             dma((2,)),
             dma((4,)),

time: 165 us -> 155 us (0.939)
  Pallas kernels: 156 us -> 146 us
    pallas_call x1, Pallas kernels: 156 us -> 146 us  [fused(): pl.pallas_call(functools.partial(fused_kernel, capacity), out_shape=[jax....]
where the time goes in v2:
time: 155 us
  Pallas kernels  146 us (94%)
  local copies, waits for them, and re-layouts  5.49 us (4%)
  other arithmetic  2.01 us (1%)
    pallas_call x1, Pallas kernels, fused(): pl.pallas_call(functools.partial(fused_kernel, capacity), out_shape=[jax....  146 us
    unnamed x5, local copies, waits for them, and re-layouts  5.49 us

profile of v2, /device:TPU:0, one launch (start us, length us, event | category | flops | bytes accessed | tf_op | source)
XLA Modules:
  0.0 154.6 jit_solution(3406151630994786481)
XLA Ops:
  0.6 0.7 fusion
  1.3 0.1 convolution_select_fusion
  1.5 0.7 select_reduce_fusion
  2.2 0.6 pad_maximum_fusion.meta_ref
  2.8 146.4 %shard_map.85 = (bf16[128,2048]{1,0:T(8,128)(2,1)}, bf16[1024,768]{1,0:T(8,128)(2,1)}, bf16[384,1024]{1,0:T(8,128)(2,1)}) custom-call(bf16[128,2048]{1,0:T(8,128)(2,1)} %tok_ref.1, bf16[128,2048]{1,0:T(8,128)(2,1)} %og_ref.1, f32[32,128]{1,0:T(8,128)} %pad_maximum_fusion.meta_ref, bf16[2048,768]{1,0:T(8,128)(2,1)} %bitcast.12, bf16[384,2048]{1,0:T(8,128)(2,1)} %bitcast.13), custom_call_target="tpu_custom_call" | custom-call | flops 11274289152 | bytes 12582912 | tf_op jit(solution)/shard_map/pallas_call | solution.py:529
  149.1 1.9 %copy.12 = bf16[128,2048]{1,0:T(8,128)(2,1)} copy(bf16[128,2048]{1,0:T(8,128)(2,1)} %get-tuple-element.12) | data formatting | bytes 1048576
  151.0 0.0 copy-start
  151.0 2.7 %copy.13 = bf16[1,1024,768]{2,1,0:T(8,128)(2,1)} copy(bf16[1,1024,768]{2,1,0:T(8,128)(2,1)} %bitcast.7) | data formatting | bytes 3145728
  153.8 0.0 copy-done
  153.8 0.9 copy.14
Async XLA Ops:
  151.0 2.7 %copy-start = (bf16[384,1024]{1,0:T(8,128)(2,1)S(1)}, bf16[384,1024]{1,0:T(8,128)(2,1)}, u32[]{:S(2)}) copy-start(bf16[384,1024]{1,0:T(8,128)(2,1)} %get-tuple-element.8) | copy-start | bytes 2359300

commit v3 on v2

--- a/solution.py
+++ b/solution.py
@@ -286,14 +286,6 @@
                     arrive(other, far)
                     pass_on(other, 4, far, partner).start()
 
-    for a in range(2):
-
-        @pl.when(jnp.logical_not(is_inner))
-        def _():
-            arrive(a, far)
-
-        dispatch(a, 3)
-
     def arrive_rows(a, b):
         for d in range(1, INNER):
             for piece in range(len(pieces)):
@@ -385,11 +377,19 @@
     hidden_rows(0)
     for c in range(quarters):
         input_rows(0, c)
+
+    for a in range(2):
+
+        @pl.when(jnp.logical_not(is_inner))
+        def _():
+            arrive(a, far)
+
+        dispatch(a, 3)
+
+    early = ((3, 0), (3, 1))
     arrive_rows(0, 1)
     joined_rows(1)
     arrive_rows(1, 1)
-    early = [(3, c) for c in range(quarters // 2)]
-    late = [(d, c) for c in range(quarters) for d in (3, 1, 2) if (d, c) not in early]
     for d, c in early:
         back_copy(0, d, c).start()
     hidden_rows(1)
@@ -397,8 +397,6 @@
         input_rows(1, c)
         for d in (3, 1, 2):
             back_copy(1, d, c).start()
-    for d, c in late:
-        back_copy(0, d, c).start()
 
     half_width = width // 2
     tile = 256
@@ -430,6 +428,9 @@
     for c in range(quarters):
         for d in range(1, INNER):
             back_copy(1, d, c).wait_recv()
+        for d in (3, 1, 2):
+            if (d, c) not in early:
+                back_copy(0, d, c).start()
         totals = [combine(1, half, c) for half in range(2)]
 
         @pl.when(is_inner)
@@ -507,6 +508,32 @@
         copy.wait_send()
     for copy in stores:
         copy.wait()
+
+
+def settle_kernel(parts, *refs):
+    held, given, sems = refs[: len(refs) // 2], refs[len(refs) // 2 : -1], refs[-1]
+    copies = []
+    for k, (src, dst) in enumerate(zip(held, given)):
+        size = src.shape[0] // parts
+        for i in range(parts):
+            at = pl.ds(i * size, size)
+            copies.append(pltpu.make_async_copy(src.at[at], dst.at[at], sems.at[k, i]))
+    for copy in copies:
+        copy.start()
+    for copy in copies:
+        copy.wait()
+
+
+def settle(*arrays):
+    parts = 4
+    hbm = pl.BlockSpec(memory_space=pl.ANY)
+    return pl.pallas_call(
+        functools.partial(settle_kernel, parts),
+        out_shape=[jax.ShapeDtypeStruct(a.shape, a.dtype) for a in arrays],
+        in_specs=[hbm] * len(arrays),
+        out_specs=[hbm] * len(arrays),
+        scratch_shapes=[pltpu.SemaphoreType.DMA((len(arrays), parts))],
+    )(*arrays)
 
 
 def fused(capacity, tokens, out_grad, expert_ids, gate_weights, w_in, w_out):
@@ -580,6 +607,7 @@
             flops=2 * slots * width * ff * 8, bytes_accessed=12 * 2**20, transcendentals=slots * ff
         ),
     )(tokens, out_grad, meta, w_in[0], w_out[0])
+    token_grad, grad_in, grad_out = settle(token_grad, grad_in, grad_out)
     return token_grad, grad_in[None], grad_out[None]
 
 

time: 155 us -> 238 us (1.54)
  Pallas kernels: 146 us -> 235 us
  local copies, waits for them, and re-layouts: 5.49 us -> 0 us
    pallas_call x0 -> x1, Pallas kernels: none -> 88.6 us  [settle(): pl.pallas_call(functools.partial(settle_kernel, parts), out_shape=[jax.Sh...]
    unnamed x5 -> x0, local copies, waits for them, and re-layouts: 5.49 us -> none
where the time goes in v3:
time: 238 us
  Pallas kernels  235 us (99%)
    pallas_call x1, Pallas kernels, fused(): pl.pallas_call(functools.partial(fused_kernel, capacity), out_shape=[jax....  146 us
    pallas_call x1, Pallas kernels, settle(): pl.pallas_call(functools.partial(settle_kernel, parts), out_shape=[jax.Sh...  88.6 us

profile of v3, /device:TPU:0, one launch (start us, length us, event | category | flops | bytes accessed | tf_op | source)
XLA Modules:
  0.0 237.7 jit_solution(2552082928096910303)
XLA Ops:
  0.6 0.7 fusion
  1.3 0.1 convolution_select_fusion
  1.5 0.7 select_reduce_fusion
  2.2 0.6 pad_maximum_fusion.meta_ref
  2.8 146.4 %shard_map.85 = (bf16[128,2048]{1,0:T(8,128)(2,1)}, bf16[1024,768]{1,0:T(8,128)(2,1)}, bf16[384,1024]{1,0:T(8,128)(2,1)}) custom-call(bf16[128,2048]{1,0:T(8,128)(2,1)} %tok_ref.1, bf16[128,2048]{1,0:T(8,128)(2,1)} %og_ref.1, f32[32,128]{1,0:T(8,128)} %pad_maximum_fusion.meta_ref, bf16[2048,768]{1,0:T(8,128)(2,1)} %bitcast.10, bf16[384,2048]{1,0:T(8,128)(2,1)} %bitcast.11), custom_call_target="tpu_custom_call" | custom-call | flops 11274289152 | bytes 12582912 | tf_op jit(solution)/shard_map/pallas_call | solution.py:556
  149.1 88.6 %shard_map.86 = (bf16[128,2048]{1,0:T(8,128)(2,1)}, bf16[1024,768]{1,0:T(8,128)(2,1)}, bf16[384,1024]{1,0:T(8,128)(2,1)}) custom-call(bf16[128,2048]{1,0:T(8,128)(2,1)} %get-tuple-element.9.refs_0_, bf16[1024,768]{1,0:T(8,128)(2,1)} %get-tuple-element.10.refs_1_, bf16[384,1024]{1,0:T(8,128)(2,1)} %get-tuple-element.11.refs_2_), custom_call_target="tpu_custom_call" | custom-call | tf_op jit(solution)/shard_map/pallas_call | solution.py:530

commit v4 on v3

--- a/solution.py
+++ b/solution.py
@@ -330,9 +330,14 @@
             preferred_element_type=jnp.float32,
         ).astype(jnp.bfloat16)
 
-    def back_copy(b, d, c):
-        at = (pl.ds(b * block_rows + d * rows, rows), pl.ds(c * wide, wide))
-        return remote(d_rows.at[at], ret.at[at], r_send.at[b, d, c], r_recv.at[b, d, c], pdev(d))
+    back_own, back_pair, back_far = range(3)
+
+    def back_copy(piece, d, c):
+        b, start, size = ((0, 0, ready), (0, ready, rows - ready), (1, 0, rows))[piece]
+        at = (pl.ds(b * block_rows + d * rows + start, size), pl.ds(c * wide, wide))
+        return remote(
+            d_rows.at[at], ret.at[at], r_send.at[piece, d, c], r_recv.at[piece, d, c], pdev(d)
+        )
 
     from_end_near, from_end_far, from_partner, from_cross, from_cross_far = range(5)
 
@@ -360,9 +365,10 @@
         cols = pl.ds(c * wide, wide)
         total = jnp.zeros((count, wide), jnp.float32)
         for d in range(INNER):
-            at = pl.ds(b * block_rows + d * rows, rows)
+            start = ready if (b, half) == (0, 1) else 0
+            at = pl.ds(b * block_rows + d * rows + start, rows - start)
             total = total + lax.dot_general(
-                chosen(s, half, d).astype(jnp.bfloat16),
+                chosen(s, half, d)[start:].astype(jnp.bfloat16),
                 (ret if d else d_rows)[at, cols],
                 (((0,), (0,)), ((), ())),
                 preferred_element_type=jnp.float32,
@@ -391,12 +397,12 @@
     joined_rows(1)
     arrive_rows(1, 1)
     for d, c in early:
-        back_copy(0, d, c).start()
+        back_copy(back_pair, d, c).start()
     hidden_rows(1)
     for c in range(quarters):
         input_rows(1, c)
         for d in (3, 1, 2):
-            back_copy(1, d, c).start()
+            back_copy(back_far, d, c).start()
 
     half_width = width // 2
     tile = 256
@@ -427,10 +433,10 @@
 
     for c in range(quarters):
         for d in range(1, INNER):
-            back_copy(1, d, c).wait_recv()
+            back_copy(back_far, d, c).wait_recv()
         for d in (3, 1, 2):
             if (d, c) not in early:
-                back_copy(0, d, c).start()
+                back_copy(back_pair, d, c).start()
         totals = [combine(1, half, c) for half in range(2)]
 
         @pl.when(is_inner)
@@ -442,6 +448,10 @@
         def _():
             for k in range(2):
                 send_part(totals[k], k, from_end_near + k, partner, c)
+
+    for c in range(quarters):
+        for d in (3, 1, 2):
+            back_copy(back_own, d, c).start()
 
     for copy in swaps:
         copy.wait_recv()
@@ -459,7 +469,7 @@
 
     for c in range(quarters):
         for d in range(1, INNER):
-            back_copy(0, d, c).wait_recv()
+            back_copy(back_pair, d, c).wait_recv()
         total = combine(0, 1, c)
 
         @pl.when(is_inner)
@@ -469,12 +479,12 @@
         @pl.when(jnp.logical_not(is_inner))
         def _():
             send_part(total, 2, from_partner, partner, c)
-
-        kept[:, pl.ds(c * wide, wide)] = combine(0, 0, c)
 
     for c in range(quarters):
         cols = pl.ds(c * wide, wide)
-        kept[:, cols] += landed(from_partner, c)
+        for d in range(1, INNER):
+            back_copy(back_own, d, c).wait_recv()
+        kept[:, cols] = combine(0, 0, c) + landed(from_partner, c)
 
         @pl.when(is_inner)
         def _():
@@ -501,38 +511,30 @@
         for a in range(2):
             for piece in range(len(pieces)):
                 plane_copy(a, piece, d).wait_send()
-        for b in range(2):
+        for piece in range(3):
             for c in range(quarters):
-                back_copy(b, d, c).wait_send()
+                back_copy(piece, d, c).wait_send()
     for copy in swaps:
         copy.wait_send()
     for copy in stores:
         copy.wait()
 
 
-def settle_kernel(parts, *refs):
-    held, given, sems = refs[: len(refs) // 2], refs[len(refs) // 2 : -1], refs[-1]
-    copies = []
-    for k, (src, dst) in enumerate(zip(held, given)):
-        size = src.shape[0] // parts
-        for i in range(parts):
-            at = pl.ds(i * size, size)
-            copies.append(pltpu.make_async_copy(src.at[at], dst.at[at], sems.at[k, i]))
-    for copy in copies:
-        copy.start()
-    for copy in copies:
-        copy.wait()
+def settle_kernel(*refs):
+    half = len(refs) // 2
+    for src, dst in zip(refs[:half], refs[half:]):
+        dst[...] = src[...]
 
 
 def settle(*arrays):
     parts = 4
-    hbm = pl.BlockSpec(memory_space=pl.ANY)
+    specs = [pl.BlockSpec((a.shape[0] // parts, a.shape[1]), lambda i: (i, 0)) for a in arrays]
     return pl.pallas_call(
-        functools.partial(settle_kernel, parts),
+        settle_kernel,
+        grid=(parts,),
         out_shape=[jax.ShapeDtypeStruct(a.shape, a.dtype) for a in arrays],
-        in_specs=[hbm] * len(arrays),
-        out_specs=[hbm] * len(arrays),
-        scratch_shapes=[pltpu.SemaphoreType.DMA((len(arrays), parts))],
+        in_specs=specs,
+        out_specs=specs,
     )(*arrays)
 
 
@@ -592,8 +594,8 @@
             dma((PLANES,)),
             dma((2, 4, INNER)),
             dma((2, 4, INNER)),
-            dma((2, INNER, quarters)),
-            dma((2, INNER, quarters)),
+            dma((3, INNER, quarters)),
+            dma((3, INNER, quarters)),
             dma((3, quarters)),
             dma((5, quarters)),
             dma((2,)),

time: 238 us -> 151 us (0.63)
  Pallas kernels: 235 us -> 148 us
    pallas_call x1, Pallas kernels: 88.6 us -> 4.05 us  [settle(): pl.pallas_call(settle_kernel, grid=(parts,), out_shape=[jax.ShapeDtypeStr...]
where the time goes in v4:
time: 151 us
  Pallas kernels  148 us (98%)
  other arithmetic  2.01 us (1%)
    pallas_call x1, Pallas kernels, fused(): pl.pallas_call(functools.partial(fused_kernel, capacity), out_shape=[jax....  144 us
    pallas_call x1, Pallas kernels, settle(): pl.pallas_call(settle_kernel, grid=(parts,), out_shape=[jax.ShapeDtypeStr...  4.05 us

profile of v4, /device:TPU:0, one launch (start us, length us, event | category | flops | bytes accessed | tf_op | source)
XLA Modules:
  0.0 151.1 jit_solution(4264708108035523353)
XLA Ops:
  0.6 0.7 fusion
  1.3 0.1 convolution_select_fusion
  1.5 0.7 select_reduce_fusion
  2.2 0.6 pad_maximum_fusion.meta_ref
  2.8 144.3 %shard_map.85 = (bf16[128,2048]{1,0:T(8,128)(2,1)}, bf16[1024,768]{1,0:T(8,128)(2,1)}, bf16[384,1024]{1,0:T(8,128)(2,1)}) custom-call(bf16[128,2048]{1,0:T(8,128)(2,1)} %tok_ref.1, bf16[128,2048]{1,0:T(8,128)(2,1)} %og_ref.1, f32[32,128]{1,0:T(8,128)} %pad_maximum_fusion.meta_ref, bf16[2048,768]{1,0:T(8,128)(2,1)} %bitcast.10, bf16[384,2048]{1,0:T(8,128)(2,1)} %bitcast.11), custom_call_target="tpu_custom_call" | custom-call | flops 11274289152 | bytes 12582912 | tf_op jit(solution)/shard_map/pallas_call | solution.py:558
  147.1 4.0 %shard_map.86 = (bf16[128,2048]{1,0:T(8,128)(2,1)}, bf16[1024,768]{1,0:T(8,128)(2,1)}, bf16[384,1024]{1,0:T(8,128)(2,1)}) custom-call(bf16[128,2048]{1,0:T(8,128)(2,1)} %get-tuple-element.9.refs_0_, bf16[1024,768]{1,0:T(8,128)(2,1)} %get-tuple-element.10.refs_1_, bf16[384,1024]{1,0:T(8,128)(2,1)} %get-tuple-element.11.refs_2_), custom_call_target="tpu_custom_call" | custom-call | tf_op jit(solution)/shard_map/pallas_call | solution.py:532

commit v5 on v4

--- a/solution.py
+++ b/solution.py
@@ -188,7 +188,6 @@
     for copy in loads:
         copy.start()
     ztok[z] = tok_ref[...]
-    zog[z] = og_ref[...]
     zmeta[z] = meta_ref[...]
 
     row_id = lax.broadcasted_iota(jnp.int32, (rows, count), 0).astype(jnp.float32)
@@ -247,6 +246,7 @@
                 plane_copy(a, piece, d).start()
 
     dispatch(0, 0)
+    zog[z] = og_ref[...]
     dispatch(1, 0)
 
     arrive(0, partner)
@@ -527,7 +527,7 @@
 
 
 def settle(*arrays):
-    parts = 4
+    parts = 2
     specs = [pl.BlockSpec((a.shape[0] // parts, a.shape[1]), lambda i: (i, 0)) for a in arrays]
     return pl.pallas_call(
         settle_kernel,

time: 151 us -> 150 us (level)
  no operation moved by 1% of the time
where the time goes in v5:
time: 150 us
  Pallas kernels  147 us (98%)
  other arithmetic  2.01 us (1%)
    pallas_call x1, Pallas kernels, fused(): pl.pallas_call(functools.partial(fused_kernel, capacity), out_shape=[jax....  144 us

profile of v5, /device:TPU:0, one launch (start us, length us, event | category | flops | bytes accessed | tf_op | source)
XLA Modules:
  0.0 150.0 jit_solution(6041907446631205707)
XLA Ops:
  0.6 0.7 fusion
  1.3 0.1 convolution_select_fusion
  1.5 0.7 select_reduce_fusion
  2.2 0.6 pad_maximum_fusion.meta_ref
  2.8 144.3 %shard_map.85 = (bf16[128,2048]{1,0:T(8,128)(2,1)}, bf16[1024,768]{1,0:T(8,128)(2,1)}, bf16[384,1024]{1,0:T(8,128)(2,1)}) custom-call(bf16[128,2048]{1,0:T(8,128)(2,1)} %tok_ref.1, bf16[128,2048]{1,0:T(8,128)(2,1)} %og_ref.1, f32[32,128]{1,0:T(8,128)} %pad_maximum_fusion.meta_ref, bf16[2048,768]{1,0:T(8,128)(2,1)} %bitcast.10, bf16[384,2048]{1,0:T(8,128)(2,1)} %bitcast.11), custom_call_target="tpu_custom_call" | custom-call | flops 11274289152 | bytes 12582912 | tf_op jit(solution)/shard_map/pallas_call | solution.py:558
  147.1 3.0 %shard_map.86 = (bf16[128,2048]{1,0:T(8,128)(2,1)}, bf16[1024,768]{1,0:T(8,128)(2,1)}, bf16[384,1024]{1,0:T(8,128)(2,1)}) custom-call(bf16[128,2048]{1,0:T(8,128)(2,1)} %get-tuple-element.9.refs_0_, bf16[1024,768]{1,0:T(8,128)(2,1)} %get-tuple-element.10.refs_1_, bf16[384,1024]{1,0:T(8,128)(2,1)} %get-tuple-element.11.refs_2_), custom_call_target="tpu_custom_call" | custom-call | tf_op jit(solution)/shard_map/pallas_call | solution.py:532
